TPU v7x, 32 devices: a whole 2x2x4 slice. The times are simulated.
32 devices in a mesh: groups: 2 (over x), tensor: 16 (over z, y, core).
Axes of the slice: x: 2, y: 2, z: 4, core: 2. Of those that a mesh axis runs over, the one named last changes fastest.
Arguments:
- hidden: bfloat16 [512, 8192], P('groups', 'tensor'), parts along dimension 0, may hold values from -6 to 6
- attention_norm_gain: bfloat16 [8192], replicated, may hold values from 0.099609375 to 1.8984375
- query_weight: bfloat16 [8192, 8192], P(None, 'tensor'), may hold values from -0.0625 to 0.0625
- key_value_weight: bfloat16 [8192, 2048], P(None, 'tensor'), may hold values from -0.0625 to 0.0625
- output_weight: bfloat16 [8192, 8192], P(None, 'tensor'), may hold values from -0.5 to 0.5
- adapter_down_factors: bfloat16 [64, 8192, 64], P(None, 'tensor'), may hold values from -0.0625 to 0.0625
- adapter_query_up: bfloat16 [64, 64, 8192], P(None, None, 'tensor'), may hold values from -0.75 to 0.75
- adapter_key_value_up: bfloat16 [64, 64, 2048], P(None, None, 'tensor'), may hold values from -0.75 to 0.75
- output_adapter_down: bfloat16 [64, 8192, 64], P(None, 'tensor'), may hold values from -0.5 to 0.5
- output_adapter_up: bfloat16 [64, 64, 8192], P(None, None, 'tensor'), may hold values from -0.75 to 0.75
- key_cache: bfloat16 [4096, 512, 128], P(('groups', 'tensor')), parts along dimension 0, as said below
- value_cache: bfloat16 [4096, 512, 128], P(('groups', 'tensor')), parts along dimension 0, may hold values from -6 to 6
- adapter: int32 [512, 1], P('groups'), parts along dimension 0, may hold values from 0 to 63
- lengths: int32 [512], P('groups'), parts along dimension 0, may hold values from 1 to 512, as said below
Outputs:
- result: bfloat16 [512, 8192], P('groups', 'tensor'), parts along dimension 0
There are 2 independent parts, one for each index of `groups`. A program takes and returns all parts, laid end to end along the dimension named above; an argument that names none is the same for every part. Nothing has to cross between parts.
Inputs may be any that keep to these rules, and one draw needn't show every extreme that they name: Each row attends to its first lengths positions of the cache and to its new token, which stands at position lengths; some row has exactly 512 and some row 1. Every adapter serves at least one row. `key_cache`: keys are stored already rotated.
All inputs are finite; a program needn't handle non-finite values.
Results may differ from a plain program's by a relative error of at most 0.007.
The roundings to bfloat16 on the way count: a program that leaves them out, or rounds other values in their place, can miss the bound.
Values may be sent and summed in bfloat16 or wider, within the bound.
A program may use at most 192 MiB of HBM per device.

v0:
```python
import jax
import jax.numpy as jnp
from jax import lax
from jax.sharding import PartitionSpec as P

QUERY_HEADS = 64
KEY_VALUE_HEADS = 8
HEAD_SIZE = 128


adapter_scale = 0.5
rope_base = 500000.0
norm_eps = 1e-05


def rotate(values, positions):
    half_width = values.shape[-1] // 2
    frequency = rope_base ** (-(jnp.arange(half_width, dtype=jnp.float32) * 2.0) / values.shape[-1])
    angles = positions.astype(jnp.float32)[:, None, None] * frequency[None, None, :]
    cosine = jnp.cos(angles)
    sinus_part = jnp.sin(angles)
    front = values[..., :half_width]
    behind = values[..., half_width:]
    return jnp.concatenate(
        [front * cosine - behind * sinus_part, front * sinus_part + behind * cosine], axis=-1
    )


def project_down(inputs, table, chosen_adapter):
    spread = jnp.einsum("rd,adk->rak", inputs, table, preferred_element_type=jnp.float32)
    return jnp.sum(jnp.where(chosen_adapter[:, :, None], spread, 0.0), axis=1)


def project_upward(low_values, table, chosen_adapter):
    expanded = jnp.where(
        chosen_adapter[:, :, None], low_values[:, None, :], jnp.zeros((), low_values.dtype)
    )
    return jnp.einsum("rak,akc->rc", expanded, table, preferred_element_type=jnp.float32)


def body(
    hidden,
    attention_norm_gain,
    query_weight,
    key_value_weight,
    output_weight,
    adapter_down_factors,
    adapter_query_up,
    adapter_key_value_up,
    output_adapter_down,
    output_adapter_up,
    key_cache,
    value_cache,
    adapter,
    lengths,
):
    dev_count = lax.axis_size("tensor")
    device = lax.axis_index("tensor")
    row_count = hidden.shape[0]
    adapter_table = adapter_down_factors.shape[0]
    chosen_adapter = adapter == jnp.arange(adapter_table, dtype=jnp.int32)[None, :]
    stream = lax.all_gather(hidden, "tensor", axis=1, tiled=True).astype(jnp.float32)
    mean_square = jnp.mean(stream * stream, axis=1, keepdims=True)
    normed_input = (
        stream
        * lax.rsqrt(mean_square + norm_eps)
        * attention_norm_gain.astype(jnp.float32)[None, :]
    ).astype(jnp.bfloat16)
    input_span = adapter_down_factors.shape[1]
    normed_slice = lax.dynamic_slice_in_dim(normed_input, device * input_span, input_span, 1)
    reduced_input = lax.psum(
        project_down(normed_slice, adapter_down_factors, chosen_adapter), "tensor"
    ).astype(jnp.bfloat16)
    query_cols = jnp.dot(
        normed_input, query_weight, preferred_element_type=jnp.float32
    ) + adapter_scale * project_upward(reduced_input, adapter_query_up, chosen_adapter)
    query_cols = (
        rotate(query_cols.reshape(row_count, -1, HEAD_SIZE), lengths)
        .reshape(row_count, -1)
        .astype(jnp.bfloat16)
    )
    key_value_columns = jnp.dot(
        normed_input, key_value_weight, preferred_element_type=jnp.float32
    ) + adapter_scale * project_upward(reduced_input, adapter_key_value_up, chosen_adapter)
    key_value_columns = key_value_columns.astype(jnp.bfloat16)
    row_blocks = dev_count // KEY_VALUE_HEADS
    block_rows = row_count // row_blocks
    kv_group = device // row_blocks
    row_block = device % row_blocks
    group_heads = QUERY_HEADS // KEY_VALUE_HEADS
    query_all, kv_all = (
        lax.all_gather(query_cols, "tensor", axis=1, tiled=True),
        lax.all_gather(key_value_columns, "tensor", axis=1, tiled=True),
    )
    query_rows = lax.dynamic_slice_in_dim(query_all, row_block * block_rows, block_rows, 0).reshape(
        block_rows, group_heads, KEY_VALUE_HEADS, HEAD_SIZE
    )
    queries = lax.dynamic_slice_in_dim(query_rows, kv_group, 1, 2)[:, :, 0, :]
    kv_block = lax.dynamic_slice(
        kv_all, (row_block * block_rows, kv_group * 2 * HEAD_SIZE), (block_rows, 2 * HEAD_SIZE)
    )
    block_lengths = lax.dynamic_slice_in_dim(lengths, row_block * block_rows, block_rows, 0)
    new_key = rotate(kv_block[:, :HEAD_SIZE].astype(jnp.float32)[:, None, :], block_lengths)[
        :, 0, :
    ].astype(jnp.bfloat16)
    new_value = kv_block[:, HEAD_SIZE:]
    factor = HEAD_SIZE ** (-0.5)
    scores = (
        jnp.einsum("rgd,rpd->rgp", queries, key_cache, preferred_element_type=jnp.float32) * factor
    )
    cache_len = key_cache.shape[1]
    live = jnp.arange(cache_len, dtype=jnp.int32)[None, :] < block_lengths[:, None]
    scores = jnp.where(live[:, None, :], scores, -jnp.inf)
    own_score = (
        jnp.einsum("rgd,rd->rg", queries, new_key, preferred_element_type=jnp.float32) * factor
    )
    highest = jnp.maximum(jnp.max(scores, axis=2), own_score)
    weights = jnp.exp(scores - highest[:, :, None])
    own_weight = jnp.exp(own_score - highest)
    weight_sum = jnp.sum(weights, axis=2) + own_weight
    probs = (weights / weight_sum[:, :, None]).astype(jnp.bfloat16)
    own_prob = (own_weight / weight_sum).astype(jnp.bfloat16)
    head_out = jnp.einsum("rgp,rpd->rgd", probs, value_cache, preferred_element_type=jnp.float32)
    head_out = (
        head_out
        + own_prob.astype(jnp.float32)[:, :, None] * new_value.astype(jnp.float32)[:, None, :]
    )
    block_out = head_out.reshape(block_rows, group_heads * HEAD_SIZE).astype(jnp.bfloat16)
    all_blocks = lax.all_gather(block_out, "tensor", axis=0, tiled=True)
    attended_rows = jnp.transpose(
        all_blocks.reshape(KEY_VALUE_HEADS, row_blocks, block_rows, -1), (1, 2, 0, 3)
    ).reshape(row_count, -1)
    output_span = output_adapter_down.shape[1]
    attended_slice = lax.dynamic_slice_in_dim(attended_rows, device * output_span, output_span, 1)
    reduced_output = lax.psum(
        project_down(attended_slice, output_adapter_down, chosen_adapter), "tensor"
    ).astype(jnp.bfloat16)
    block_output = hidden.astype(jnp.float32) + jnp.dot(
        attended_rows, output_weight, preferred_element_type=jnp.float32
    )
    block_output = block_output + adapter_scale * project_upward(
        reduced_output, output_adapter_up, chosen_adapter
    )
    return block_output.astype(jnp.bfloat16)


def solution(mesh):
    placed = (
        P("groups", "tensor"),
        P(),
        P(None, "tensor"),
        P(None, "tensor"),
        P(None, "tensor"),
        P(None, "tensor", None),
        P(None, None, "tensor"),
        P(None, None, "tensor"),
        P(None, "tensor", None),
        P(None, None, "tensor"),
        P(("groups", "tensor"), None, None),
        P(("groups", "tensor"), None, None),
        P("groups", None),
        P("groups"),
    )
    return jax.shard_map(
        body, mesh=mesh, in_specs=placed, out_specs=P("groups", "tensor"), check_vma=False
    )
```

profile of v0, /device:TPU:0, one launch (start us, length us, event | category | flops | bytes accessed | tf_op | source)
XLA Modules:
  0.0 379.4 jit_solution(2559741781077108079)
XLA Ops:
  6.5 0.7 all-gather.5.cloned.1.call-update
  7.3 0.7 convert_element_type.59
  8.0 0.7 convert_element_type.62
  8.7 0.7 iota_compare_fusion.1
  9.4 56.0 %all-gather.5.cloned.1.call-done = bf16[256,8192]{1,0:T(8,128)(2,1)} async-done(((bf16[256,512]{1,0:T(8,128)(2,1)}), bf16[256,8192]{1,0:T(8,128)(2,1)}) %all-gather.5.cloned.1.call-update) | async-done | bytes 4194320 | tf_op jit(solution)/shard_map/all_gather | solution.py:62
  65.5 3.3 fusion
  68.9 1.2 fusion.2
  70.1 1.1 copy-done.5
  71.2 1.3 fusion.58
  72.5 0.7 select_reduce_fusion.1
  73.2 59.0 %psum.14 = bf16[256,64]{0,1:T(8,128)(2,1)S(1)} all-reduce(f32[256,64]{0,1:T(8,128)S(1)} %select_reduce_fusion.1), channel_id=1, replica_groups=mesh['groups'=2,'tensor'=16] {'tensor'}, use_global_device_ids=true, to_apply=%region_2.3 | all-reduce | flops 16384 | bytes 98304 | tf_op jit(solution)/shard_map/psum | solution.py:71
  132.2 1.9 fusion.39
  134.7 2.2 fusion.42
  137.5 7.2 %fusion.80 = f32[256,512]{1,0:T(8,128)S(1)} fusion(bf16[256,8192]{1,0:T(8,128)(2,1)} %copy-done.2, bf16[8192,512]{1,0:T(8,128)(2,1)} %param.16), kind=kOutput, calls=%fused_computation.93 | convolution fusion | flops 2147483648 | bytes 13107200 | tf_op jit(solution)/shard_map/dot_general | solution.py:74
  144.7 1.3 fusion.26
  147.0 0.9 copy.29
  148.4 23.7 %all-gather.9.cloned.1.call-done = bf16[256,2048]{0,1:T(8,128)(2,1)} async-done(((bf16[256,128]{0,1:T(8,128)(2,1)}), bf16[256,2048]{0,1:T(8,128)(2,1)}) %all-gather.9.cloned.1.call-update) | async-done | bytes 1048592 | tf_op jit(solution)/shard_map/all_gather | solution.py:93
  172.1 0.8 dynamic-slice_convert_fusion
  173.3 50.5 %all-gather.7.cloned.1.call-done = bf16[256,8192]{0,1:T(8,128)(2,1)} async-done(((bf16[256,512]{0,1:T(8,128)(2,1)}), bf16[256,8192]{0,1:T(8,128)(2,1)}) %all-gather.7.cloned.1.call-update) | async-done | bytes 4194320 | tf_op jit(solution)/shard_map/all_gather | solution.py:92
  223.8 1.7 constant_dynamic-slice_fusion.1
  226.2 8.1 %fusion.12 = (f32[128,8]{1,0:T(8,128)S(1)}, f32[128,8,512]{2,1,0:T(8,128)S(1)}) fusion(pred[128,512]{1,0:T(8,128)(4,1)S(1)} %iota_compare_fusion, bf16[128,512,128]{2,1,0:T(8,128)(2,1)} %param.24, bf16[128,8,1,128]{3,1,0,2:T(8,128)(2,1)S(1)} %copy.30), kind=kOutput, calls=%fused_computation.19 | convolution fusion | flops 135789568 | bytes 19206144 | tf_op jit(solution)/shard_map/rgd,rpd->rgp/dot_general | solution.py:109
  234.6 0.8 fusion.13
  235.6 7.3 %fusion.35 = bf16[128,8,128]{2,1,0:T(8,128)(2,1)S(1)} fusion(bf16[128,512,128]{2,1,0:T(8,128)(2,1)} %param.25, f32[128,8,512]{2,1,0:T(8,128)S(1)} %get-tuple-element.18, f32[128,8]{1,0:T(8,128)S(1)} %copy.36, f32[128,8]{1,0:T(8,128)S(1)} %copy.34, pred[128,512]{1,0:T(8,128)(4,1)S(1)} %iota_compare_fusion, f32[128,128]{1,0:T(8,128)S(1)} %copy.38, ...), kind=kOutput, calls=%fused_computation.30 | convolution fusion | flops 137232384 | bytes 19279872 | tf_op jit(solution)/shard_map/rgp,rpd->rgd/dot_general | solution.py:123
  242.9 0.8 copy.53
  243.7 49.2 %all-gather.11.cloned.1.call-done = bf16[2048,1024]{1,0:T(8,128)(2,1)} async-done(((bf16[128,1024]{1,0:T(8,128)(2,1)}), bf16[2048,1024]{1,0:T(8,128)(2,1)}) %all-gather.11.cloned.1.call-update) | async-done | bytes 4194320 | tf_op jit(solution)/shard_map/all_gather | solution.py:129
  292.9 4.5 %copy.39 = bf16[2,128,8,1024]{3,2,1,0:T(8,128)(2,1)S(1)} copy(bf16[2,128,8,1024]{3,1,0,2:T(8,128)(2,1)} %bitcast.77) | data formatting | bytes 8388608 | tf_op jit(solution)/shard_map/transpose | solution.py:130
  297.4 4.4 %copy.51 = bf16[32,8,8,1024]{3,1,2,0:T(8,128)(2,1)S(1)} copy(bf16[32,8,8,1024]{3,2,1,0:T(8,128)(2,1)S(1)} %bitcast.72) | data formatting | bytes 8388608
  301.8 1.3 fusion.56
  303.8 0.7 select_reduce_fusion
  304.4 59.2 %psum.15 = bf16[256,64]{0,1:T(8,128)(2,1)S(1)} all-reduce(f32[256,64]{0,1:T(8,128)S(1)} %select_reduce_fusion), channel_id=1, replica_groups=mesh['groups'=2,'tensor'=16] {'tensor'}, use_global_device_ids=true, to_apply=%region_6.7 | all-reduce | flops 16384 | bytes 98304 | tf_op jit(solution)/shard_map/psum | solution.py:135
  363.7 7.1 %convolution_add_fusion.1 = f32[256,512]{1,0:T(8,128)S(1)} fusion(bf16[256,8192]{1,0:T(8,128)(2,1)} %bitcast.76, bf16[8192,512]{1,0:T(8,128)(2,1)} %param.18, bf16[256,512]{1,0:T(8,128)(2,1)S(1)} %copy-done.8), kind=kOutput, calls=%fused_computation.28 | convolution fusion | flops 2147745792 | bytes 13369344 | tf_op jit(solution)/shard_map/dot_general | solution.py:138
  370.8 2.0 fusion.32
  (55 shorter events, 5.1 us)
Async XLA Ops:
  6.5 127.6 %copy-start = (bf16[8192,128]{1,0:T(8,128)(2,1)S(1)}, bf16[8192,128]{1,0:T(8,128)(2,1)}, u32[]{:S(2)}) copy-start(bf16[8192,128]{1,0:T(8,128)(2,1)} %param.17) | copy-start | bytes 6291460
  6.5 58.9 %all-gather.5.cloned.1.call-start = ((), (), s32[]{:S(2)}) async-start(), calls=%async_computation | async-start | bytes 4456448 | tf_op jit(solution)/shard_map/all_gather | solution.py:62
  7.3 164.8 %all-gather.9.cloned.1.call-start = ((), (), s32[]{:S(2)}) async-start(), calls=%async_computation.2 | async-start | bytes 1114112 | tf_op jit(solution)/shard_map/all_gather | solution.py:93
  65.5 3.4 copy-start.4
  68.9 2.3 copy-start.5
  70.1 2.4 copy-start.2
  132.2 2.5 copy-start.3
  136.9 86.9 %all-gather.7.cloned.1.call-start = ((), (), s32[]{:S(2)}) async-start(), calls=%async_computation.1 | async-start | bytes 4456448 | tf_op jit(solution)/shard_map/all_gather | solution.py:92
  137.5 7.2 %copy-start.10 = (bf16[64,64,512]{2,1,0:T(8,128)(2,1)S(1)}, bf16[64,64,512]{2,1,0:T(8,128)(2,1)}, u32[]{:S(2)}) copy-start(bf16[64,64,512]{2,1,0:T(8,128)(2,1)} %param.20) | copy-start | bytes 12582916
  146.0 2.2 copy-start.9
  147.9 145.0 %all-gather.11.cloned.1.call-start = ((), (), s32[]{:S(2)}) async-start(), calls=%async_computation.3 | async-start | bytes 4456448 | tf_op jit(solution)/shard_map/all_gather | solution.py:129
  297.4 4.4 %copy-start.6 = (bf16[64,512,64]{1,2,0:T(8,128)(2,1)S(1)}, bf16[64,512,64]{1,2,0:T(8,128)(2,1)}, u32[]{:S(2)}) copy-start(bf16[64,512,64]{1,2,0:T(8,128)(2,1)} %param.22) | copy-start | bytes 12582916
  301.8 1.9 copy-start.7
  303.8 59.9 %copy-start.8 = (bf16[256,512]{1,0:T(8,128)(2,1)S(1)}, bf16[256,512]{1,0:T(8,128)(2,1)}, u32[]{:S(2)}) copy-start(bf16[256,512]{1,0:T(8,128)(2,1)} %param.14) | copy-start | bytes 786436
  363.7 7.1 %copy-start.11 = (bf16[64,64,512]{2,1,0:T(8,128)(2,1)S(1)}, bf16[64,64,512]{2,1,0:T(8,128)(2,1)}, u32[]{:S(2)}) copy-start(bf16[64,64,512]{2,1,0:T(8,128)(2,1)} %param.23) | copy-start | bytes 12582916
  363.7 9.1 %copy-start.1 = (bf16[8192,128]{1,0:T(8,128)(2,1)S(1)}, bf16[8192,128]{1,0:T(8,128)(2,1)}, u32[]{:S(2)}) copy-start(bf16[8192,128]{1,0:T(8,128)(2,1)} %param.17) | copy-start | bytes 6291460
Sparse Core Ops, SparseCore 0:
  9.5 55.9 all-gather.4
  137.0 35.0 all-gather.8
  174.3 49.4 all-gather.6
  243.8 49.0 all-gather.10
where the time goes:
time: 380 us; the launch traced here: 379 us
  waiting for transfers between devices  180 us (47%)
  blocking collectives  118 us (31%)
  matrix products  39.7 us (10%)
  local copies, waits for them, and re-layouts  16.1 us (4%)
  between operations  13.5 us (4%)
  other arithmetic  11.4 us (3%)
    psum x1, blocking collectives, body(): lax.psum(project_down(attended_slice, output_adapter_down, chosen_adapter...  59.2 us
    psum x1, blocking collectives, body(): lax.psum(project_down(normed_slice, adapter_down_factors, chosen_adapter)...  59 us
    all_gather x1, waiting for transfers between devices, body(): lax.all_gather(hidden, 'tensor', axis=1, tiled=True).astype(jnp.float32)  56 us
    all_gather x1, waiting for transfers between devices, body(): lax.all_gather(query_cols, 'tensor', axis=1, tiled=True)  50.5 us
    all_gather x1, waiting for transfers between devices, body(): all_blocks = lax.all_gather(block_out, 'tensor', axis=0, tiled=True)  49.2 us
    all_gather x1, waiting for transfers between devices, body(): lax.all_gather(key_value_columns, 'tensor', axis=1, tiled=True)  23.7 us
    dot_general x1, matrix products, body(): jnp.einsum('rgd,rpd->rgp', queries, key_cache, preferred_element_type=jnp...  8.13 us
    unnamed x29, local copies, waits for them, and re-layouts  7.93 us
  transfers between devices with their start and end apart: 4, of which 4 were waited for; matrix products, arithmetic and copies ran while one was open for 4% of the time, Pallas kernels for 0%

commit v1 on v0

v1 whole, which is shorter than its diff:
```python
import functools

import jax
import jax.numpy as jnp
from jax import lax
from jax.experimental import pallas as pl
from jax.experimental.pallas import tpu as pltpu
from jax.sharding import PartitionSpec as P

QUERY_HEADS = 64
KEY_VALUE_HEADS = 8
HEAD_SIZE = 128
GROUP_HEADS = QUERY_HEADS // KEY_VALUE_HEADS

adapter_scale = 0.5
rope_base = 500000.0
norm_eps = 1e-05

MESH = pl.DeviceIdType.MESH
F32 = jnp.float32
BF16 = jnp.bfloat16
NT = (((1,), (1,)), ((), ()))


def remote(src, dst, send_sem, recv_sem, peer):
    return pltpu.make_async_remote_copy(
        src_ref=src,
        dst_ref=dst,
        send_sem=send_sem,
        recv_sem=recv_sem,
        device_id={"tensor": peer},
        device_id_type=MESH,
    )


def greet_all(n, me):
    barrier = pltpu.get_barrier_semaphore()

    def greet(i, carry):
        pl.semaphore_signal(
            barrier, inc=1, device_id={"tensor": lax.rem(me + i, n)}, device_id_type=MESH
        )
        return carry

    lax.fori_loop(1, n, greet, 0)
    pl.semaphore_wait(barrier, n - 1)


def for_peers(n, me, action):
    def step(i, carry):
        action(i, lax.rem(me + i, n))
        return carry

    lax.fori_loop(1, n, step, 0)


class Exchange:
    def __init__(self, n, me, buf, send, recv, source):
        self.n, self.me, self.buf, self.send, self.recv, self.source = n, me, buf, send, recv, source

    def copy(self, i, peer):
        return remote(
            self.source(peer), self.buf.at[self.me], self.send.at[i], self.recv.at[self.me], peer
        )

    def start(self):
        for_peers(self.n, self.me, lambda i, peer: self.copy(i, peer).start())

    def wait_arrived(self):
        def arrived(i, peer):
            remote(
                self.source(peer), self.buf.at[peer], self.send.at[i], self.recv.at[peer], peer
            ).wait_recv()

        for_peers(self.n, self.me, arrived)

    def wait_sent(self):
        for_peers(self.n, self.me, lambda i, peer: self.copy(i, peer).wait_send())


class Gather:
    def __init__(self, n, me, view, zsend, ysend, csend, recv):
        self.wide = 2 if n % 4 == 0 and n <= 16 else 1
        self.depth = n // (2 * self.wide)
        self.view, self.me = view, me
        self.zsend, self.ysend, self.csend, self.recv = zsend, ysend, csend, recv
        self.core = lax.rem(me, 2)
        self.side = lax.rem(me // 2, self.wide)
        self.level = me // (2 * self.wide)

    def index(self, level, side, core):
        return (level * self.wide + side) * 2 + core

    def copy(self, block, send_sem, peer):
        return remote(self.view(block), self.view(block), send_sem, self.recv.at[block], peer)

    def up(self, d):
        block = self.index(self.level - d, self.side, self.core)
        return self.copy(block, self.zsend.at[0, d], self.index(self.level + 1, self.side, self.core))

    def down(self, d):
        block = self.index(self.level + d, self.side, self.core)
        return self.copy(block, self.zsend.at[1, d], self.index(self.level - 1, self.side, self.core))

    def across(self, level, sem):
        block = self.index(level, self.side, self.core)
        return self.copy(block, self.ysend.at[sem], self.index(self.level, 1 - self.side, self.core))

    def over(self, level, side, sem):
        block = self.index(level, side, self.core)
        return self.copy(
            block, self.csend.at[side, sem], self.index(self.level, self.side, 1 - self.core)
        )

    def await_block(self, block, peer):
        self.copy(block, self.zsend.at[0, 0], peer).wait_recv()

    def each_sign(self, d, action):
        @pl.when(self.level - d >= 0)
        def _():
            action(self.level - d, 0)

        @pl.when((d > 0) & (self.level + d < self.depth))
        def _():
            action(self.level + d, 1)

    def line(self, d):
        def low(level, sign):
            @pl.when(d > 0)
            def _():
                other = self.level - 1 if sign == 0 else self.level + 1
                self.await_block(
                    self.index(level, self.side, self.core),
                    self.index(other, self.side, self.core),
                )

            if sign == 0:

                @pl.when(self.level + 1 < self.depth)
                def _():
                    self.up(d).start()

                @pl.when((d == 0) & (self.level > 0))
                def _():
                    self.down(d).start()

            else:

                @pl.when(self.level > 0)
                def _():
                    self.down(d).start()

            if self.wide == 2:
                self.across(level, 2 * d + sign).start()
            self.over(level, self.side, 2 * d + sign).start()

        self.each_sign(d, low)

    def rest(self, d):
        def take(level, sign):
            if self.wide == 2:
                self.await_block(
                    self.index(level, 1 - self.side, self.core),
                    self.index(self.level, 1 - self.side, self.core),
                )
                self.over(level, 1 - self.side, 2 * d + sign).start()

        self.each_sign(d, take)

        def other(level, sign):
            for side in range(self.wide):
                self.await_block(
                    self.index(level, side, 1 - self.core),
                    self.index(self.level, self.side, 1 - self.core),
                )

        self.each_sign(d, other)

    def wait_sent(self):
        def step(d, carry):
            def sent(level, sign):
                if sign == 0:

                    @pl.when(self.level + 1 < self.depth)
                    def _():
                        self.up(d).wait_send()

                    @pl.when((d == 0) & (self.level > 0))
                    def _():
                        self.down(d).wait_send()

                else:

                    @pl.when(self.level > 0)
                    def _():
                        self.down(d).wait_send()

                if self.wide == 2:
                    self.across(level, 2 * d + sign).wait_send()
                for side in range(self.wide):
                    self.over(level, side, 2 * d + sign).wait_send()

            self.each_sign(d, sent)
            return carry

        lax.fori_loop(0, self.depth, step, 0)

    def each_chip(self, d, action):
        def step(i, carry):
            level = jnp.where(i < self.wide, self.level - d, self.level + d)
            side = lax.rem(i, self.wide)

            @pl.when((level >= 0) & (level < self.depth) & ((i < self.wide) | (d > 0)))
            def _():
                action(level * self.wide + side)

            return carry

        lax.fori_loop(0, 2 * self.wide, step, 0)


def gather_semaphores(n):
    return [
        pltpu.SemaphoreType.DMA((2, n)),
        pltpu.SemaphoreType.DMA((2 * n,)),
        pltpu.SemaphoreType.DMA((2, 2 * n)),
        pltpu.SemaphoreType.DMA((n,)),
    ]


def low_partial(values, down, adapter, low):
    rank = HEAD_SIZE // 2
    lanes = lax.broadcasted_iota(jnp.int32, (values.shape[0], HEAD_SIZE), 1) // rank
    low[...] = jnp.zeros_like(low)
    width = 4 * HEAD_SIZE

    def step(i, carry):
        spread = lax.dot_general(
            values, down[pl.ds(pl.multiple_of(i * width, width), width), :], NT,
            preferred_element_type=F32,
        )
        total = low[...]
        for part in range(width // HEAD_SIZE):
            mine = adapter == lanes + (i * (width // rank) + part * (HEAD_SIZE // rank))
            total = total + jnp.where(mine, spread[:, part * HEAD_SIZE : (part + 1) * HEAD_SIZE], 0.0)
        low[...] = total
        return carry

    lax.fori_loop(0, down.shape[0] // width, step, 0)


def low_upward(low, tables, adapter, totals):
    rank = HEAD_SIZE // 2
    lanes = lax.broadcasted_iota(jnp.int32, low.shape, 1) // rank
    width = 4 * HEAD_SIZE

    def step(i, carry):
        parts = []
        for part in range(width // HEAD_SIZE):
            mine = adapter == lanes + (i * (width // rank) + part * (HEAD_SIZE // rank))
            parts.append(jnp.where(mine, low, 0.0).astype(BF16))
        spread = jnp.concatenate(parts, axis=1)
        at = pl.ds(pl.multiple_of(i * width, width), width)
        for table, total in zip(tables, totals):
            total[...] += adapter_scale * jnp.dot(spread, table[at, :], preferred_element_type=F32)
        return carry

    lax.fori_loop(0, tables[0].shape[0] // width, step, 0)


def reduce_low(n, me, pieces, low_all):
    total = pieces[0]
    for i in range(1, n):
        total = total + pieces[i]
    total = total + pltpu.roll(total, HEAD_SIZE // 2, 1)
    low_all[me] = total.astype(BF16).astype(F32)


def project_kernel(
    n,
    hidden, gain, adapter, cosine, sine, wq_hbm, wkv_hbm, down_hbm, upq_hbm, upkv_hbm,
    q_out, kv_out,
    buf, wq, wkv, down, upq, upkv, acc_q, acc_kv, stat, inv, own, low, pieces, low_all, q_cut, kv_cut,
    load_sem, zsend, ysend, csend, grecv, st_send, st_recv, rs_send, rs_recv, lo_send, lo_recv,
    q_send, q_recv, kv_send, kv_recv,
):
    me = lax.axis_index("tensor")
    rows, span = hidden.shape
    loads = [
        pltpu.make_async_copy(src, dst, load_sem.at[i])
        for i, (src, dst) in enumerate(
            [(down_hbm, down), (wq_hbm, wq), (wkv_hbm, wkv), (upq_hbm, upq), (upkv_hbm, upkv)]
        )
    ]
    buf[me] = hidden[...]
    greet_all(n, me)
    gather = Gather(n, me, lambda block: buf.at[block], zsend, ysend, csend, grecv)
    gather.line(0)
    for load in loads:
        load.start()

    own_values = hidden[...].astype(F32)
    squares = jnp.sum(own_values * own_values, axis=1, keepdims=True)
    stat[me] = jnp.transpose(jnp.broadcast_to(squares, (rows, HEAD_SIZE)))[:8, :]
    stats = Exchange(n, me, stat, st_send, st_recv, lambda peer: stat.at[me])
    stats.start()
    acc_q[...] = jnp.zeros_like(acc_q)
    acc_kv[...] = jnp.zeros_like(acc_kv)
    stats.wait_arrived()
    total = stat[0]
    for i in range(1, n):
        total = total + stat[i]
    mean = total[0:1, :] / (n * span)
    scale = lax.rsqrt(mean + norm_eps)
    inv[...] = jnp.transpose(jnp.broadcast_to(scale, (HEAD_SIZE, rows)))

    def normed(block):
        return (
            buf[block].astype(F32) * inv[:, 0:1] * gain[block].astype(F32)
        ).astype(BF16)

    who = adapter[...]
    own[...] = normed(me)
    loads[0].wait()
    low_partial(own[...], down, who, low)
    piece = rows // n
    pieces[me] = low[pl.ds(pl.multiple_of(me * piece, 8), piece), :]
    reduce = Exchange(
        n, me, pieces, rs_send, rs_recv,
        lambda peer: low.at[pl.ds(pl.multiple_of(peer * piece, 8), piece), :],
    )
    reduce.start()
    spread = Exchange(n, me, low_all, lo_send, lo_recv, lambda peer: low_all.at[me])
    loads[1].wait()
    loads[2].wait()
    loads[3].wait()
    loads[4].wait()

    def step(d, carry):
        @pl.when(d + 1 < gather.depth)
        def _():
            gather.line(d + 1)

        @pl.when(d == 1)
        def _():
            reduce.wait_arrived()
            reduce_low(n, me, pieces, low_all)
            spread.start()

        @pl.when(d == 2)
        def _():
            spread.wait_arrived()
            low_upward(low_all[...].reshape(rows, HEAD_SIZE), [upq, upkv], who, [acc_q, acc_kv])

        gather.rest(d)

        def chip_part(chip):
            for core in range(2):
                block = chip * 2 + core
                values = normed(block)
                at = pl.ds(pl.multiple_of(block * span, span), span)
                acc_q[...] += jnp.dot(values, wq[at, :], preferred_element_type=F32)
                acc_kv[...] += jnp.dot(values, wkv[at, :], preferred_element_type=F32)

        gather.each_chip(d, chip_part)
        return carry

    lax.fori_loop(0, gather.depth, step, 0)

    row_blocks = n // KEY_VALUE_HEADS
    block_rows = rows // row_blocks
    slots = acc_q.shape[1] // HEAD_SIZE
    cos, sin = cosine[...], sine[...]
    kv_cut[...] = acc_kv[...].astype(BF16)
    kv_group = me // row_blocks

    def kv_copy(part):
        peer = kv_group * row_blocks + part
        slot = lax.rem(me, row_blocks)
        return peer, slot, remote(
            kv_cut.at[pl.ds(part * block_rows, block_rows), :], kv_out.at[slot],
            kv_send.at[part], kv_recv.at[slot], peer,
        )

    def q_copy(i, part):
        column = me * slots + i
        peer = lax.rem(column, KEY_VALUE_HEADS) * row_blocks + part
        slot = column // KEY_VALUE_HEADS
        return peer, slot, remote(
            q_cut.at[i, pl.ds(part * block_rows, block_rows), :], q_out.at[slot],
            q_send.at[i, part], q_recv.at[slot], peer,
        )

    for part in range(row_blocks):
        peer, slot, copy = kv_copy(part)

        @pl.when(peer != me)
        def _():
            copy.start()

        @pl.when(peer == me)
        def _():
            kv_out[slot] = kv_cut[pl.ds(part * block_rows, block_rows), :]

    for i in range(slots):
        values = acc_q[:, i * HEAD_SIZE : (i + 1) * HEAD_SIZE]
        q_cut[i] = (values * cos + pltpu.roll(values, HEAD_SIZE // 2, 1) * sin).astype(BF16)
        for part in range(row_blocks):
            peer, slot, copy = q_copy(i, part)

            @pl.when(peer != me)
            def _():
                copy.start()

            @pl.when(peer == me)
            def _():
                q_out[slot] = q_cut[i, pl.ds(part * block_rows, block_rows), :]

    stats.wait_sent()
    reduce.wait_sent()
    spread.wait_sent()
    gather.wait_sent()
    for part in range(row_blocks):
        peer, slot, copy = kv_copy(part)

        @pl.when(peer != me)
        def _():
            copy.wait_send()
            remote(
                kv_cut.at[pl.ds(part * block_rows, block_rows), :], kv_out.at[part],
                kv_send.at[part], kv_recv.at[part], peer,
            ).wait_recv()

    for i in range(slots):
        for part in range(row_blocks):
            peer, slot, copy = q_copy(i, part)

            @pl.when(peer != me)
            def _():
                copy.wait_send()

    for slot in range(GROUP_HEADS):
        sender = (slot * KEY_VALUE_HEADS + kv_group) // slots

        @pl.when(sender != me)
        def _():
            remote(
                q_cut.at[0, pl.ds(0, block_rows), :], q_out.at[slot],
                q_send.at[0, 0], q_recv.at[slot], sender,
            ).wait_recv()


def output_kernel(
    n,
    hidden, attended, adapter, wo_hbm, down_hbm, up_hbm,
    result,
    buf, wo, down, up, acc, low, pieces, low_all,
    load_sem, zsend, ysend, csend, grecv, rs_send, rs_recv, lo_send, lo_recv,
):
    me = lax.axis_index("tensor")
    rows, span = hidden.shape
    block_rows, width = attended.shape
    row_blocks = rows // block_rows
    loads = [
        pltpu.make_async_copy(src, dst, load_sem.at[i])
        for i, (src, dst) in enumerate([(down_hbm, down), (wo_hbm, wo), (up_hbm, up)])
    ]
    for load in loads:
        load.start()

    def at_block(block):
        return (
            block // row_blocks,
            pl.ds(pl.multiple_of(lax.rem(block, row_blocks) * block_rows, block_rows), block_rows),
        )

    kv_group, own_rows = at_block(me)
    buf[kv_group, own_rows, :] = attended[...]
    acc[...] = hidden[...].astype(F32)
    greet_all(n, me)

    def view(block):
        group, at = at_block(block)
        return buf.at[group, at, :]

    gather = Gather(n, me, view, zsend, ysend, csend, grecv)
    gather.line(0)
    who = adapter[...]
    piece = rows // n
    reduce = Exchange(
        n, me, pieces, rs_send, rs_recv,
        lambda peer: low.at[pl.ds(pl.multiple_of(peer * piece, 8), piece), :],
    )
    spread = Exchange(n, me, low_all, lo_send, lo_recv, lambda peer: low_all.at[me])

    def first_low():
        first = pl.multiple_of(lax.rem(me, row_blocks) * span, span)
        low_partial(buf[kv_group, :, pl.ds(first, span)], down, who, low)
        pieces[me] = low[pl.ds(pl.multiple_of(me * piece, 8), piece), :]
        reduce.start()

    def second_low():
        reduce.wait_arrived()
        reduce_low(n, me, pieces, low_all)
        spread.start()

    def third_low():
        spread.wait_arrived()
        low_upward(low_all[...].reshape(rows, HEAD_SIZE), [up], who, [acc])

    early = row_blocks == 2
    for load in loads:
        load.wait()

    def step(d, carry):
        @pl.when(d + 1 < gather.depth)
        def _():
            gather.line(d + 1)

        if early:
            pl.when(d == 1)(second_low)
            pl.when(d == 2)(third_low)
        gather.rest(d)
        if early:
            pl.when(d == 0)(first_low)

        def chip_part(chip):
            block = chip * 2
            group = block // row_blocks
            first = pl.multiple_of(lax.rem(block, row_blocks) * block_rows, block_rows)
            at = pl.ds(first, 2 * block_rows)
            acc[at, :] += jnp.dot(
                buf[group, at, :], wo[pl.ds(pl.multiple_of(group * width, width), width), :],
                preferred_element_type=F32,
            )

        gather.each_chip(d, chip_part)
        return carry

    lax.fori_loop(0, gather.depth, step, 0)
    if not early:
        first_low()
        second_low()
        third_low()
    result[...] = acc[...].astype(BF16)
    reduce.wait_sent()
    spread.wait_sent()
    gather.wait_sent()


def rotate_tables(positions):
    half_width = HEAD_SIZE // 2
    frequency = rope_base ** (-(jnp.arange(half_width, dtype=F32) * 2.0) / HEAD_SIZE)
    angles = positions.astype(F32)[:, None] * frequency[None, :]
    cosine, sine = jnp.cos(angles), jnp.sin(angles)
    return (
        jnp.concatenate([cosine, cosine], axis=1),
        jnp.concatenate([-sine, sine], axis=1),
    )


def in_vmem():
    return pl.BlockSpec(memory_space=pltpu.VMEM)


def anywhere():
    return pl.BlockSpec(memory_space=pl.ANY)


def body(
    hidden,
    attention_norm_gain,
    query_weight,
    key_value_weight,
    output_weight,
    adapter_down_factors,
    adapter_query_up,
    adapter_key_value_up,
    output_adapter_down,
    output_adapter_up,
    key_cache,
    value_cache,
    adapter,
    lengths,
):
    n = lax.axis_size("tensor")
    device = lax.axis_index("tensor")
    rows, span = hidden.shape
    kv_width = key_value_weight.shape[1]
    row_blocks = n // KEY_VALUE_HEADS
    block_rows = rows // row_blocks
    slots = span // HEAD_SIZE
    dma = pltpu.SemaphoreType.DMA
    cosine, sine = rotate_tables(lengths)

    def low_table(table):
        return jnp.swapaxes(table, 1, 2).reshape(-1, table.shape[1])

    def up_table(table):
        return table.reshape(-1, table.shape[2])

    low_rows = adapter_down_factors.shape[0] * adapter_down_factors.shape[2]
    width = query_weight.shape[0]
    low_scratch = [
        pltpu.VMEM((rows, HEAD_SIZE), F32),
        pltpu.VMEM((n, rows // n, HEAD_SIZE), F32),
        pltpu.VMEM((n, rows // n, HEAD_SIZE), F32),
    ]
    queries, kv_pieces = pl.pallas_call(
        functools.partial(project_kernel, n),
        out_shape=(
            jax.ShapeDtypeStruct((GROUP_HEADS, block_rows, HEAD_SIZE), BF16),
            jax.ShapeDtypeStruct((row_blocks, block_rows, kv_width), BF16),
        ),
        in_specs=[in_vmem()] * 5 + [anywhere()] * 5,
        out_specs=(in_vmem(), in_vmem()),
        scratch_shapes=[
            pltpu.VMEM((n, rows, span), BF16),
            pltpu.VMEM((width, span), BF16),
            pltpu.VMEM((width, kv_width), BF16),
            pltpu.VMEM((low_rows, span), BF16),
            pltpu.VMEM((low_rows, span), BF16),
            pltpu.VMEM((low_rows, kv_width), BF16),
            pltpu.VMEM((rows, span), F32),
            pltpu.VMEM((rows, kv_width), F32),
            pltpu.VMEM((n, 8, rows), F32),
            pltpu.VMEM((rows, HEAD_SIZE), F32),
            pltpu.VMEM((rows, span), BF16),
        ]
        + low_scratch
        + [
            pltpu.VMEM((slots, rows, HEAD_SIZE), BF16),
            pltpu.VMEM((rows, kv_width), BF16),
            dma((5,)),
        ]
        + gather_semaphores(n)
        + [dma((n,))] * 6
        + [dma((slots, row_blocks)), dma((GROUP_HEADS,)), dma((row_blocks,)), dma((row_blocks,))],
        compiler_params=pltpu.CompilerParams(
            collective_id=0, has_side_effects=True, vmem_limit_bytes=44 << 20
        ),
        cost_estimate=pl.CostEstimate(
            flops=2 * rows * width * (span + kv_width), bytes_accessed=24 << 20, transcendentals=0
        ),
    )(
        hidden,
        attention_norm_gain.reshape(n, 1, span),
        adapter,
        cosine,
        sine,
        query_weight,
        key_value_weight,
        low_table(adapter_down_factors),
        up_table(adapter_query_up),
        up_table(adapter_key_value_up),
    )

    row_block = device % row_blocks
    first_row = row_block * block_rows
    kv_block = jnp.transpose(kv_pieces, (1, 0, 2)).reshape(block_rows, 2 * HEAD_SIZE)
    block_lengths = lax.dynamic_slice_in_dim(lengths, first_row, block_rows, 0)
    block_cosine = lax.dynamic_slice_in_dim(cosine, first_row, block_rows, 0)
    block_sine = lax.dynamic_slice_in_dim(sine, first_row, block_rows, 0)
    fresh_key = kv_block[:, :HEAD_SIZE].astype(F32)
    new_key = (
        fresh_key * block_cosine + jnp.roll(fresh_key, HEAD_SIZE // 2, axis=1) * block_sine
    ).astype(BF16)
    new_value = kv_block[:, HEAD_SIZE:]
    block_out = attend(queries, new_key, new_value, key_cache, value_cache, block_lengths)

    out_width = output_weight.shape[0]
    out_low_rows = output_adapter_down.shape[0] * output_adapter_down.shape[2]
    return pl.pallas_call(
        functools.partial(output_kernel, n),
        out_shape=jax.ShapeDtypeStruct((rows, span), BF16),
        in_specs=[in_vmem()] * 3 + [anywhere()] * 3,
        out_specs=in_vmem(),
        scratch_shapes=[
            pltpu.VMEM((KEY_VALUE_HEADS, rows, GROUP_HEADS * HEAD_SIZE), BF16),
            pltpu.VMEM((out_width, span), BF16),
            pltpu.VMEM((out_low_rows, span), BF16),
            pltpu.VMEM((out_low_rows, span), BF16),
            pltpu.VMEM((rows, span), F32),
        ]
        + low_scratch
        + [dma((3,))]
        + gather_semaphores(n)
        + [dma((n,))] * 4,
        compiler_params=pltpu.CompilerParams(
            collective_id=1, has_side_effects=True, vmem_limit_bytes=44 << 20
        ),
        cost_estimate=pl.CostEstimate(
            flops=2 * rows * out_width * span, bytes_accessed=20 << 20, transcendentals=0
        ),
    )(
        hidden,
        block_out,
        adapter,
        output_weight,
        low_table(output_adapter_down),
        up_table(output_adapter_up),
    )


def attend(queries, new_key, new_value, key_cache, value_cache, block_lengths):
    block_rows = new_key.shape[0]
    queries = jnp.transpose(queries, (1, 0, 2))
    factor = HEAD_SIZE ** (-0.5)
    scores = jnp.einsum("rgd,rpd->rgp", queries, key_cache, preferred_element_type=F32) * factor
    live = jnp.arange(key_cache.shape[1], dtype=jnp.int32)[None, :] < block_lengths[:, None]
    scores = jnp.where(live[:, None, :], scores, -jnp.inf)
    own_score = jnp.einsum("rgd,rd->rg", queries, new_key, preferred_element_type=F32) * factor
    highest = jnp.maximum(jnp.max(scores, axis=2), own_score)
    weights = jnp.exp(scores - highest[:, :, None])
    own_weight = jnp.exp(own_score - highest)
    weight_sum = jnp.sum(weights, axis=2) + own_weight
    probs = (weights / weight_sum[:, :, None]).astype(BF16)
    own_prob = (own_weight / weight_sum).astype(BF16)
    head_out = jnp.einsum("rgp,rpd->rgd", probs, value_cache, preferred_element_type=F32)
    head_out = head_out + own_prob.astype(F32)[:, :, None] * new_value.astype(F32)[:, None, :]
    return head_out.reshape(block_rows, GROUP_HEADS * HEAD_SIZE).astype(BF16)


def solution(mesh):
    placed = (
        P("groups", "tensor"),
        P(),
        P(None, "tensor"),
        P(None, "tensor"),
        P(None, "tensor"),
        P(None, "tensor", None),
        P(None, None, "tensor"),
        P(None, None, "tensor"),
        P(None, "tensor", None),
        P(None, None, "tensor"),
        P(("groups", "tensor"), None, None),
        P(("groups", "tensor"), None, None),
        P("groups", None),
        P("groups"),
    )
    return jax.shard_map(
        body, mesh=mesh, in_specs=placed, out_specs=P("groups", "tensor"), check_vma=False
    )
```

time: 380 us -> 126 us (0.33)
  waiting for transfers between devices: 180 us -> 0 us
  blocking collectives: 118 us -> 0 us
  Pallas kernels: 0 us -> 97.3 us
  matrix products: 39.7 us -> 15.9 us
  between operations: 13.5 us -> 0.16 us
  other arithmetic: 11.4 us -> 2.39 us
  local copies, waits for them, and re-layouts: 16.1 us -> 10.3 us
    all_gather x4 -> x0, waiting for transfers between devices: 179 us -> none  [the longest x1 56 us: body(): lax.all_gather(hidden, 'tensor', axis=1, tiled=True).astype(jnp.float32)]
    psum x2 -> x0, blocking collectives: 118 us -> none  [the longest x1 59.2 us: body(): lax.psum(project_down(attended_slice, output_adapter_down, chosen_adapter...]
    pallas_call x0 -> x2, Pallas kernels: none -> 97.3 us  [the longest x1 54.3 us: body(): pl.pallas_call(functools.partial(project_kernel, n), out_shape=(jax.Shape...]
    dot_general x8 -> x3, matrix products: 37.1 us -> 15.9 us  [the longest x1 8.16 us: attend(): jnp.einsum('rgd,rpd->rgp', queries, key_cache, preferred_element_type=F32)]
    reduce_sum x4 -> x1, other arithmetic: 5.35 us -> 0.75 us  [attend(): weight_sum = jnp.sum(weights, axis=2) + own_weight]
    transpose x1 -> x0, local copies, waits for them, and re-layouts: 4.51 us -> none  [body(): jnp.transpose(all_blocks.reshape(KEY_VALUE_HEADS, row_blocks, block_rows,...]
    unnamed x29 -> x17, local copies, waits for them, and re-layouts: 7.93 us -> 8.24 us
  transfers between devices with their start and end apart: 4 -> 0, of which waited for: 4 -> 0; matrix products, arithmetic and copies ran while one was open for 4% -> 0% of each run, Pallas kernels for 0% -> 0%
where the time goes in v1:
time: 126 us
  Pallas kernels  97.3 us (77%)
  matrix products  15.9 us (13%)
  local copies, waits for them, and re-layouts  10.3 us (8%)
  other arithmetic  2.39 us (2%)
    pallas_call x1, Pallas kernels, body(): pl.pallas_call(functools.partial(project_kernel, n), out_shape=(jax.Shape...  54.3 us
    pallas_call x1, Pallas kernels, body(): pl.pallas_call(functools.partial(output_kernel, n), out_shape=jax.ShapeDt...  42.9 us
    unnamed x17, local copies, waits for them, and re-layouts  8.24 us
    dot_general x1, matrix products, attend(): jnp.einsum('rgd,rpd->rgp', queries, key_cache, preferred_element_type=F32)  8.16 us
    dot_general x1, matrix products, attend(): jnp.einsum('rgp,rpd->rgd', probs, value_cache, preferred_element_type=F32)  7.44 us

profile of v1, /device:TPU:0, one launch (start us, length us, event | category | flops | bytes accessed | tf_op | source)
XLA Modules:
  0.0 126.0 jit_solution(2073473982198653704)
XLA Ops:
  0.0 0.8 dynamic_slice.9
  0.8 0.7 convert_element_type.26
  1.4 0.7 reshape.61.gain
  2.2 0.1 iota_compare_fusion
  2.3 0.8 copy.33.adapter
  3.1 0.5 fusion.19
  3.6 0.1 pad_maximum_fusion
  3.8 0.0 copy-start
  3.8 2.2 %copy-done = bf16[64,512,64]{1,2,0:T(8,128)(2,1)S(1)} copy-done((bf16[64,512,64]{1,2,0:T(8,128)(2,1)S(1)}, bf16[64,512,64]{1,2,0:T(8,128)(2,1)}, u32[]{:S(2)}) %copy-start) | copy-done | bytes 4194328
  6.0 1.6 %copy-done.3 = bf16[8192,128]{1,0:T(8,128)(2,1)S(1)} copy-done((bf16[8192,128]{1,0:T(8,128)(2,1)S(1)}, bf16[8192,128]{1,0:T(8,128)(2,1)}, u32[]{:S(2)}) %copy-start.3) | copy-done | bytes 2097176
  7.6 0.9 copy-done.4
  8.5 1.2 copy-done.6
  9.8 54.3 %shard_map.136 = (bf16[8,128,128]{2,1,0:T(8,128)(2,1)S(1)}, bf16[2,128,128]{2,1,0:T(8,128)(2,1)S(1)}) custom-call(bf16[256,512]{1,0:T(8,128)(2,1)S(1)} %copy-done.4, bf16[16,1,512]{2,1,0:T(2,128)(2,1)S(1)} %reshape.61.gain, s32[256,1]{1,0:T(8,128)S(1)} %copy.33.adapter, f32[256,128]{1,0:T(8,128)S(1)} %get-tuple-element.20.cosine, ...), custom_call_target="tpu_custom_call" | custom-call | flops 2684354560 | bytes 25165824 | tf_op jit(solution)/shard_map/pallas_call | solution.py:609
  64.1 0.1 fusion.26
  64.2 0.1 fusion.20
  64.3 0.3 fusion.8
  64.6 0.1 copy.43
  64.7 8.2 %fusion = (f32[128,8]{1,0:T(8,128)S(1)}, f32[128,8,512]{2,1,0:T(8,128)S(1)}) fusion(pred[128,512]{1,0:T(8,128)(4,1)S(1)} %iota_compare_fusion, bf16[128,512,128]{2,1,0:T(8,128)(2,1)} %param.24, bf16[128,8,128]{2,0,1:T(8,128)(2,1)S(1)} %bitcast.46), kind=kOutput, calls=%fused_computation.3 | convolution fusion | flops 135789568 | bytes 19206144 | tf_op jit(solution)/shard_map/rgd,rpd->rgp/dot_general | solution.py:709
  72.8 0.1 copy.36
  72.9 0.1 copy.37
  73.0 0.8 fusion.1
  73.8 0.1 copy.40
  74.0 0.1 copy.39
  74.1 0.0 copy-start.1
  74.1 0.0 copy-start.2
  74.1 0.0 copy-start.5
  74.1 7.4 %fusion.2 = bf16[128,8,128]{2,1,0:T(8,128)(2,1)S(1)} fusion(bf16[128,512,128]{2,1,0:T(8,128)(2,1)} %param.25, f32[128,8,512]{2,1,0:T(8,128)S(1)} %get-tuple-element.19, f32[128,8]{1,0:T(8,128)S(1)} %copy.39, f32[128,8]{1,0:T(8,128)S(1)} %copy.37, pred[128,512]{1,0:T(8,128)(4,1)S(1)} %iota_compare_fusion, f32[128,128]{1,0:T(8,128)S(1)} %get-tuple-element.9, ...), kind=kOutput, calls=%fused_computation.6 | convolution fusion | flops 137232384 | bytes 19279872 | tf_op jit(solution)/shard_map/rgp,rpd->rgd/dot_general | solution.py:719
  81.6 0.0 copy-done.1
  81.6 0.7 copy-done.2
  82.3 0.0 copy-done.5
  82.3 42.9 %shard_map.137 = bf16[256,512]{1,0:T(8,128)(2,1)S(1)} custom-call(bf16[256,512]{1,0:T(8,128)(2,1)S(1)} %copy-done.5, bf16[128,1024]{1,0:T(8,128)(2,1)S(1)} %bitcast.43, s32[256,1]{1,0:T(8,128)S(1)} %copy.33.adapter, bf16[8192,512]{1,0:T(8,128)(2,1)} %wo_hbm.1, bf16[4096,512]{1,0:T(8,128)(2,1)S(1)} %bitcast.41, bf16[4096,512]{1,0:T(8,128)(2,1)S(1)} %bitcast.42), custom_call_target="tpu_custom_call" | custom-call | flops 2147483648 | bytes 20971520 | tf_op jit(solution)/shard_map/pallas_call | solution.py:673
  125.3 0.7 copy.58
  (10 shorter events, 0.1 us)
Async XLA Ops:
  3.8 2.2 %copy-start = (bf16[64,512,64]{1,2,0:T(8,128)(2,1)S(1)}, bf16[64,512,64]{1,2,0:T(8,128)(2,1)}, u32[]{:S(2)}) copy-start(bf16[64,512,64]{1,2,0:T(8,128)(2,1)} %param.19) | copy-start | bytes 12582916
  6.0 1.6 %copy-start.3 = (bf16[8192,128]{1,0:T(8,128)(2,1)S(1)}, bf16[8192,128]{1,0:T(8,128)(2,1)}, u32[]{:S(2)}) copy-start(bf16[8192,128]{1,0:T(8,128)(2,1)} %wkv_hbm.1) | copy-start | bytes 6291460
  7.6 0.9 copy-start.4
  8.5 1.2 copy-start.6
  74.1 7.5 %copy-start.1 = (bf16[64,512,64]{1,2,0:T(8,128)(2,1)S(1)}, bf16[64,512,64]{1,2,0:T(8,128)(2,1)}, u32[]{:S(2)}) copy-start(bf16[64,512,64]{1,2,0:T(8,128)(2,1)} %param.22) | copy-start | bytes 12582916
  74.1 8.3 %copy-start.2 = (bf16[64,64,512]{2,1,0:T(8,128)(2,1)S(1)}, bf16[64,64,512]{2,1,0:T(8,128)(2,1)}, u32[]{:S(2)}) copy-start(bf16[64,64,512]{2,1,0:T(8,128)(2,1)} %param.23) | copy-start | bytes 12582916
  74.1 8.2 %copy-start.5 = (bf16[256,512]{1,0:T(8,128)(2,1)S(1)}, bf16[256,512]{1,0:T(8,128)(2,1)}, u32[]{:S(2)}) copy-start(bf16[256,512]{1,0:T(8,128)(2,1)} %hidden.3) | copy-start | bytes 786436

commit v2 on v1

--- a/solution.py
+++ b/solution.py
@@ -278,9 +278,10 @@
 
 def project_kernel(
     n,
-    hidden, gain, adapter, cosine, sine, wq_hbm, wkv_hbm, down_hbm, upq_hbm, upkv_hbm,
-    q_out, kv_out,
-    buf, wq, wkv, down, upq, upkv, acc_q, acc_kv, stat, inv, own, low, pieces, low_all, q_cut, kv_cut,
+    hidden, gain, adapter, cosine, sine, block_cosine, block_sine, block_lengths,
+    wq_hbm, wkv_hbm, down_hbm, upq_hbm, upkv_hbm, keys_hbm, values_hbm,
+    block_out,
+    q_out, kv_out, keys, values_ref, q_rows, new_keys, new_values, heads_out, buf, wq, wkv, down, upq, upkv, acc_q, acc_kv, stat, inv, own, low, pieces, low_all, q_cut, kv_cut,
     load_sem, zsend, ysend, csend, grecv, st_send, st_recv, rs_send, rs_recv, lo_send, lo_recv,
     q_send, q_recv, kv_send, kv_recv,
 ):
@@ -289,7 +290,8 @@
     loads = [
         pltpu.make_async_copy(src, dst, load_sem.at[i])
         for i, (src, dst) in enumerate(
-            [(down_hbm, down), (wq_hbm, wq), (wkv_hbm, wkv), (upq_hbm, upq), (upkv_hbm, upkv)]
+            [(down_hbm, down), (wq_hbm, wq), (wkv_hbm, wkv), (upq_hbm, upq), (upkv_hbm, upkv),
+             (keys_hbm, keys), (values_hbm, values_ref)]
         )
     ]
     buf[me] = hidden[...]
@@ -448,6 +450,47 @@
                 q_cut.at[0, pl.ds(0, block_rows), :], q_out.at[slot],
                 q_send.at[0, 0], q_recv.at[slot], sender,
             ).wait_recv()
+
+    fresh = jnp.concatenate([kv_out[i] for i in range(row_blocks)], axis=1).astype(F32)
+    fresh_key = fresh[:, :HEAD_SIZE]
+    new_keys[...] = (
+        fresh_key * block_cosine[...]
+        + pltpu.roll(fresh_key, HEAD_SIZE // 2, 1) * block_sine[...]
+    ).astype(BF16).astype(F32)
+    new_values[...] = fresh[:, HEAD_SIZE:]
+    for slot in range(GROUP_HEADS):
+        q_rows[:, slot, :] = q_out[slot].astype(F32)
+    loads[5].wait()
+    loads[6].wait()
+    group = 8
+    cache_len = keys.shape[1]
+    place = lax.broadcasted_iota(jnp.int32, (group, GROUP_HEADS, cache_len), 2)
+    factor = HEAD_SIZE ** (-0.5)
+
+    def some_rows(i, carry):
+        at = pl.ds(pl.multiple_of(i * group, group), group)
+        queries = q_rows[at]
+        scores = factor * lax.dot_general(
+            queries.astype(BF16), keys[at], (((2,), (2,)), ((0,), (0,))),
+            preferred_element_type=F32,
+        )
+        scores = jnp.where(place < block_lengths[at], scores, -jnp.inf)
+        own_score = factor * jnp.sum(queries * new_keys[at][:, None, :], axis=2, keepdims=True)
+        highest = jnp.maximum(jnp.max(scores, axis=2, keepdims=True), own_score)
+        weights = jnp.exp(scores - highest)
+        own_weight = jnp.exp(own_score - highest)
+        share = 1.0 / (jnp.sum(weights, axis=2, keepdims=True) + own_weight)
+        heads = lax.dot_general(
+            (weights * share).astype(BF16), values_ref[at], (((2,), (1,)), ((0,), (0,))),
+            preferred_element_type=F32,
+        )
+        own_prob = (own_weight * share).astype(BF16).astype(F32)
+        heads_out[at] = heads + own_prob * new_values[at][:, None, :]
+        return carry
+
+    lax.fori_loop(0, block_rows // group, some_rows, 0)
+    for slot in range(GROUP_HEADS):
+        block_out[:, slot * HEAD_SIZE : (slot + 1) * HEAD_SIZE] = heads_out[:, slot, :].astype(BF16)
 
 
 def output_kernel(
@@ -606,15 +649,23 @@
         pltpu.VMEM((n, rows // n, HEAD_SIZE), F32),
         pltpu.VMEM((n, rows // n, HEAD_SIZE), F32),
     ]
-    queries, kv_pieces = pl.pallas_call(
+    first_row = (device % row_blocks) * block_rows
+    block_lengths = lax.dynamic_slice_in_dim(lengths, first_row, block_rows, 0)
+    block_cosine, block_sine = rotate_tables(block_lengths)
+    block_out = pl.pallas_call(
         functools.partial(project_kernel, n),
-        out_shape=(
-            jax.ShapeDtypeStruct((GROUP_HEADS, block_rows, HEAD_SIZE), BF16),
-            jax.ShapeDtypeStruct((row_blocks, block_rows, kv_width), BF16),
-        ),
-        in_specs=[in_vmem()] * 5 + [anywhere()] * 5,
-        out_specs=(in_vmem(), in_vmem()),
+        out_shape=jax.ShapeDtypeStruct((block_rows, GROUP_HEADS * HEAD_SIZE), BF16),
+        in_specs=[in_vmem()] * 8 + [anywhere()] * 7,
+        out_specs=in_vmem(),
         scratch_shapes=[
+            pltpu.VMEM((GROUP_HEADS, block_rows, HEAD_SIZE), BF16),
+            pltpu.VMEM((row_blocks, block_rows, kv_width), BF16),
+            pltpu.VMEM(key_cache.shape, BF16),
+            pltpu.VMEM(value_cache.shape, BF16),
+            pltpu.VMEM((block_rows, GROUP_HEADS, HEAD_SIZE), F32),
+            pltpu.VMEM((block_rows, HEAD_SIZE), F32),
+            pltpu.VMEM((block_rows, HEAD_SIZE), F32),
+            pltpu.VMEM((block_rows, GROUP_HEADS, HEAD_SIZE), F32),
             pltpu.VMEM((n, rows, span), BF16),
             pltpu.VMEM((width, span), BF16),
             pltpu.VMEM((width, kv_width), BF16),
@@ -631,13 +682,13 @@
         + [
             pltpu.VMEM((slots, rows, HEAD_SIZE), BF16),
             pltpu.VMEM((rows, kv_width), BF16),
-            dma((5,)),
+            dma((7,)),
         ]
         + gather_semaphores(n)
         + [dma((n,))] * 6
         + [dma((slots, row_blocks)), dma((GROUP_HEADS,)), dma((row_blocks,)), dma((row_blocks,))],
         compiler_params=pltpu.CompilerParams(
-            collective_id=0, has_side_effects=True, vmem_limit_bytes=44 << 20
+            collective_id=0, has_side_effects=True, vmem_limit_bytes=63 << 20
         ),
         cost_estimate=pl.CostEstimate(
             flops=2 * rows * width * (span + kv_width), bytes_accessed=24 << 20, transcendentals=0
@@ -648,25 +699,17 @@
         adapter,
         cosine,
         sine,
+        block_cosine,
+        block_sine,
+        block_lengths.reshape(block_rows, 1, 1),
         query_weight,
         key_value_weight,
         low_table(adapter_down_factors),
         up_table(adapter_query_up),
         up_table(adapter_key_value_up),
+        key_cache,
+        value_cache,
     )
-
-    row_block = device % row_blocks
-    first_row = row_block * block_rows
-    kv_block = jnp.transpose(kv_pieces, (1, 0, 2)).reshape(block_rows, 2 * HEAD_SIZE)
-    block_lengths = lax.dynamic_slice_in_dim(lengths, first_row, block_rows, 0)
-    block_cosine = lax.dynamic_slice_in_dim(cosine, first_row, block_rows, 0)
-    block_sine = lax.dynamic_slice_in_dim(sine, first_row, block_rows, 0)
-    fresh_key = kv_block[:, :HEAD_SIZE].astype(F32)
-    new_key = (
-        fresh_key * block_cosine + jnp.roll(fresh_key, HEAD_SIZE // 2, axis=1) * block_sine
-    ).astype(BF16)
-    new_value = kv_block[:, HEAD_SIZE:]
-    block_out = attend(queries, new_key, new_value, key_cache, value_cache, block_lengths)
 
     out_width = output_weight.shape[0]
     out_low_rows = output_adapter_down.shape[0] * output_adapter_down.shape[2]
@@ -687,7 +730,7 @@
         + gather_semaphores(n)
         + [dma((n,))] * 4,
         compiler_params=pltpu.CompilerParams(
-            collective_id=1, has_side_effects=True, vmem_limit_bytes=44 << 20
+            collective_id=1, has_side_effects=True, vmem_limit_bytes=60 << 20
         ),
         cost_estimate=pl.CostEstimate(
             flops=2 * rows * out_width * span, bytes_accessed=20 << 20, transcendentals=0
@@ -700,25 +743,6 @@
         low_table(output_adapter_down),
         up_table(output_adapter_up),
     )
-
-
-def attend(queries, new_key, new_value, key_cache, value_cache, block_lengths):
-    block_rows = new_key.shape[0]
-    queries = jnp.transpose(queries, (1, 0, 2))
-    factor = HEAD_SIZE ** (-0.5)
-    scores = jnp.einsum("rgd,rpd->rgp", queries, key_cache, preferred_element_type=F32) * factor
-    live = jnp.arange(key_cache.shape[1], dtype=jnp.int32)[None, :] < block_lengths[:, None]
-    scores = jnp.where(live[:, None, :], scores, -jnp.inf)
-    own_score = jnp.einsum("rgd,rd->rg", queries, new_key, preferred_element_type=F32) * factor
-    highest = jnp.maximum(jnp.max(scores, axis=2), own_score)
-    weights = jnp.exp(scores - highest[:, :, None])
-    own_weight = jnp.exp(own_score - highest)
-    weight_sum = jnp.sum(weights, axis=2) + own_weight
-    probs = (weights / weight_sum[:, :, None]).astype(BF16)
-    own_prob = (own_weight / weight_sum).astype(BF16)
-    head_out = jnp.einsum("rgp,rpd->rgd", probs, value_cache, preferred_element_type=F32)
-    head_out = head_out + own_prob.astype(F32)[:, :, None] * new_value.astype(F32)[:, None, :]
-    return head_out.reshape(block_rows, GROUP_HEADS * HEAD_SIZE).astype(BF16)
 
 
 def solution(mesh):

time: 126 us -> 121 us (0.960)
  matrix products: 15.9 us -> 0 us
  Pallas kernels: 97.3 us -> 112 us
  local copies, waits for them, and re-layouts: 10.3 us -> 5.22 us
  other arithmetic: 2.39 us -> 3.89 us
    dot_general x3 -> x0, matrix products: 15.9 us -> none  [the longest x1 8.16 us: attend(): jnp.einsum('rgd,rpd->rgp', queries, key_cache, preferred_element_type=F32)]
    pallas_call x1, Pallas kernels: 54.3 us -> 67.9 us  [body(): pl.pallas_call(functools.partial(project_kernel, n), out_shape=jax.ShapeD...]
    unnamed x17 -> x2, local copies, waits for them, and re-layouts: 8.24 us -> 3.14 us
    concatenate x1 -> x2, other arithmetic: 0.13 us -> 1.6 us  [rotate_tables(): jnp.concatenate([cosine, cosine], axis=1)]
where the time goes in v2:
time: 121 us
  Pallas kernels  112 us (93%)
  local copies, waits for them, and re-layouts  5.22 us (4%)
  other arithmetic  3.89 us (3%)
    pallas_call x1, Pallas kernels, body(): pl.pallas_call(functools.partial(project_kernel, n), out_shape=jax.ShapeD...  67.9 us
    pallas_call x1, Pallas kernels, body(): pl.pallas_call(functools.partial(output_kernel, n), out_shape=jax.ShapeDt...  43.9 us
    unnamed x2, local copies, waits for them, and re-layouts  3.14 us

profile of v2, /device:TPU:0, one launch (start us, length us, event | category | flops | bytes accessed | tf_op | source)
XLA Modules:
  0.0 121.0 jit_solution(12695164215131577312)
XLA Ops:
  0.0 0.8 dynamic-slice_bitcast_fusion
  0.8 0.3 fusion.1
  1.1 0.8 pad_maximum_fusion.2
  1.8 0.7 copy.20.block_lengths
  2.6 0.7 convert_element_type.6
  3.3 0.5 fusion
  3.8 0.8 pad_maximum_fusion
  4.6 1.5 %copy.19.adapter = s32[256,1]{1,0:T(8,128)} copy(s32[256,1]{0,1:T(1,128)} %param.26) | data formatting | bytes 2048 | tf_op args[12]
  6.1 1.3 %reshape.37.gain = bf16[16,1,512]{2,1,0:T(2,128)(2,1)} reshape(bf16[8192]{0:T(1024)(128)(2,1)} %param.15) | data formatting | bytes 32768 | tf_op jit(solution)/shard_map/reshape | solution.py:698
  7.5 67.9 %shard_map.136.attended = bf16[128,1024]{1,0:T(8,128)(2,1)} custom-call(bf16[256,512]{1,0:T(8,128)(2,1)} %hidden.3, bf16[16,1,512]{2,1,0:T(2,128)(2,1)} %reshape.37.gain, s32[256,1]{1,0:T(8,128)} %copy.19.adapter, f32[256,128]{1,0:T(8,128)} %get-tuple-element.13.cosine, f32[256,128]{1,0:T(8,128)} %get-tuple-element.14.sine, ...), custom_call_target="tpu_custom_call" | custom-call | flops 2684354560 | bytes 25165824 | tf_op jit(solution)/shard_map/pallas_call | solution.py:655
  75.4 43.9 %shard_map.137 = bf16[256,512]{1,0:T(8,128)(2,1)} custom-call(bf16[256,512]{1,0:T(8,128)(2,1)} %hidden.3, bf16[128,1024]{1,0:T(8,128)(2,1)} %shard_map.136.attended, s32[256,1]{1,0:T(8,128)} %copy.19.adapter, bf16[8192,512]{1,0:T(8,128)(2,1)} %wo_hbm.1, bf16[4096,512]{1,0:T(8,128)(2,1)} %bitcast.13, bf16[4096,512]{1,0:T(8,128)(2,1)} %bitcast.14), custom_call_target="tpu_custom_call" | custom-call | flops 2147483648 | bytes 20971520 | tf_op jit(solution)/shard_map/pallas_call | solution.py:716
  119.3 1.7 %copy.23 = bf16[256,512]{1,0:T(8,128)(2,1)} copy(bf16[256,512]{1,0:T(8,128)(2,1)} %shard_map.137) | data formatting | bytes 524288
  (1 shorter events, 0.0 us)

commit v3 on v2

--- a/solution.py
+++ b/solution.py
@@ -278,7 +278,7 @@
 
 def project_kernel(
     n,
-    hidden, gain, adapter, cosine, sine, block_cosine, block_sine, block_lengths,
+    hidden, gain, adapter, cosine, sine, lengths,
     wq_hbm, wkv_hbm, down_hbm, upq_hbm, upkv_hbm, keys_hbm, values_hbm,
     block_out,
     q_out, kv_out, keys, values_ref, q_rows, new_keys, new_values, heads_out, buf, wq, wkv, down, upq, upkv, acc_q, acc_kv, stat, inv, own, low, pieces, low_all, q_cut, kv_cut,
@@ -294,12 +294,12 @@
              (keys_hbm, keys), (values_hbm, values_ref)]
         )
     ]
+    for load in loads[:5]:
+        load.start()
     buf[me] = hidden[...]
     greet_all(n, me)
     gather = Gather(n, me, lambda block: buf.at[block], zsend, ysend, csend, grecv)
     gather.line(0)
-    for load in loads:
-        load.start()
 
     own_values = hidden[...].astype(F32)
     squares = jnp.sum(own_values * own_values, axis=1, keepdims=True)
@@ -318,7 +318,7 @@
 
     def normed(block):
         return (
-            buf[block].astype(F32) * inv[:, 0:1] * gain[block].astype(F32)
+            buf[block].astype(F32) * inv[:, 0:1] * gain[:, pl.ds(pl.multiple_of(block * span, span), span)].astype(F32)
         ).astype(BF16)
 
     who = adapter[...]
@@ -333,11 +333,6 @@
     )
     reduce.start()
     spread = Exchange(n, me, low_all, lo_send, lo_recv, lambda peer: low_all.at[me])
-    loads[1].wait()
-    loads[2].wait()
-    loads[3].wait()
-    loads[4].wait()
-
     def step(d, carry):
         @pl.when(d + 1 < gather.depth)
         def _():
@@ -355,6 +350,13 @@
             low_upward(low_all[...].reshape(rows, HEAD_SIZE), [upq, upkv], who, [acc_q, acc_kv])
 
         gather.rest(d)
+
+        @pl.when(d == 0)
+        def _():
+            for load in loads[1:5]:
+                load.wait()
+            for load in loads[5:]:
+                load.start()
 
         def chip_part(chip):
             for core in range(2):
@@ -451,18 +453,20 @@
                 q_send.at[0, 0], q_recv.at[slot], sender,
             ).wait_recv()
 
+    first_row = lax.rem(me, row_blocks) * block_rows
+    block_at = pl.ds(pl.multiple_of(first_row, block_rows), block_rows)
     fresh = jnp.concatenate([kv_out[i] for i in range(row_blocks)], axis=1).astype(F32)
     fresh_key = fresh[:, :HEAD_SIZE]
     new_keys[...] = (
-        fresh_key * block_cosine[...]
-        + pltpu.roll(fresh_key, HEAD_SIZE // 2, 1) * block_sine[...]
+        fresh_key * cosine[block_at, :]
+        + pltpu.roll(fresh_key, HEAD_SIZE // 2, 1) * sine[block_at, :]
     ).astype(BF16).astype(F32)
     new_values[...] = fresh[:, HEAD_SIZE:]
     for slot in range(GROUP_HEADS):
         q_rows[:, slot, :] = q_out[slot].astype(F32)
     loads[5].wait()
     loads[6].wait()
-    group = 8
+    group = 16
     cache_len = keys.shape[1]
     place = lax.broadcasted_iota(jnp.int32, (group, GROUP_HEADS, cache_len), 2)
     factor = HEAD_SIZE ** (-0.5)
@@ -474,7 +478,7 @@
             queries.astype(BF16), keys[at], (((2,), (2,)), ((0,), (0,))),
             preferred_element_type=F32,
         )
-        scores = jnp.where(place < block_lengths[at], scores, -jnp.inf)
+        scores = jnp.where(place < lengths[pl.ds(first_row + i * group, group)], scores, -jnp.inf)
         own_score = factor * jnp.sum(queries * new_keys[at][:, None, :], axis=2, keepdims=True)
         highest = jnp.maximum(jnp.max(scores, axis=2, keepdims=True), own_score)
         weights = jnp.exp(scores - highest)
@@ -552,8 +556,6 @@
         low_upward(low_all[...].reshape(rows, HEAD_SIZE), [up], who, [acc])
 
     early = row_blocks == 2
-    for load in loads:
-        load.wait()
 
     def step(d, carry):
         @pl.when(d + 1 < gather.depth)
@@ -564,6 +566,12 @@
             pl.when(d == 1)(second_low)
             pl.when(d == 2)(third_low)
         gather.rest(d)
+
+        @pl.when(d == 0)
+        def _():
+            for load in loads:
+                load.wait()
+
         if early:
             pl.when(d == 0)(first_low)
 
@@ -593,13 +601,11 @@
 
 def rotate_tables(positions):
     half_width = HEAD_SIZE // 2
-    frequency = rope_base ** (-(jnp.arange(half_width, dtype=F32) * 2.0) / HEAD_SIZE)
+    entry = jnp.arange(HEAD_SIZE, dtype=jnp.int32)
+    frequency = rope_base ** (-((entry % half_width).astype(F32) * 2.0) / HEAD_SIZE)
     angles = positions.astype(F32)[:, None] * frequency[None, :]
-    cosine, sine = jnp.cos(angles), jnp.sin(angles)
-    return (
-        jnp.concatenate([cosine, cosine], axis=1),
-        jnp.concatenate([-sine, sine], axis=1),
-    )
+    sign = jnp.where(entry < half_width, -1.0, 1.0).astype(F32)
+    return jnp.cos(angles), jnp.sin(angles) * sign[None, :]
 
 
 def in_vmem():
@@ -627,7 +633,6 @@
     lengths,
 ):
     n = lax.axis_size("tensor")
-    device = lax.axis_index("tensor")
     rows, span = hidden.shape
     kv_width = key_value_weight.shape[1]
     row_blocks = n // KEY_VALUE_HEADS
@@ -649,13 +654,10 @@
         pltpu.VMEM((n, rows // n, HEAD_SIZE), F32),
         pltpu.VMEM((n, rows // n, HEAD_SIZE), F32),
     ]
-    first_row = (device % row_blocks) * block_rows
-    block_lengths = lax.dynamic_slice_in_dim(lengths, first_row, block_rows, 0)
-    block_cosine, block_sine = rotate_tables(block_lengths)
     block_out = pl.pallas_call(
         functools.partial(project_kernel, n),
         out_shape=jax.ShapeDtypeStruct((block_rows, GROUP_HEADS * HEAD_SIZE), BF16),
-        in_specs=[in_vmem()] * 8 + [anywhere()] * 7,
+        in_specs=[in_vmem()] * 6 + [anywhere()] * 7,
         out_specs=in_vmem(),
         scratch_shapes=[
             pltpu.VMEM((GROUP_HEADS, block_rows, HEAD_SIZE), BF16),
@@ -695,13 +697,11 @@
         ),
     )(
         hidden,
-        attention_norm_gain.reshape(n, 1, span),
+        attention_norm_gain.reshape(1, n * span),
         adapter,
         cosine,
         sine,
-        block_cosine,
-        block_sine,
-        block_lengths.reshape(block_rows, 1, 1),
+        lengths.reshape(rows, 1, 1),
         query_weight,
         key_value_weight,
         low_table(adapter_down_factors),

time: 121 us -> 117 us (0.967)
  Pallas kernels: 112 us -> 109 us
  other arithmetic: 3.89 us -> 1.92 us
    pallas_call x1, Pallas kernels: 67.9 us -> 64.6 us  [body(): pl.pallas_call(functools.partial(project_kernel, n), out_shape=jax.ShapeD...]
    concatenate x2 -> x0, other arithmetic: 1.6 us -> none  [rotate_tables(): jnp.concatenate([cosine, cosine], axis=1)]
    mul x0 -> x1, other arithmetic: none -> 1.23 us  [rotate_tables(): return (jnp.cos(angles), jnp.sin(angles) * sign[None, :])]
where the time goes in v3:
time: 117 us; the launch traced here: 116 us
  Pallas kernels  109 us (93%)
  local copies, waits for them, and re-layouts  5.96 us (5%)
  other arithmetic  1.92 us (2%)
    pallas_call x1, Pallas kernels, body(): pl.pallas_call(functools.partial(project_kernel, n), out_shape=jax.ShapeD...  64.6 us
    pallas_call x1, Pallas kernels, body(): pl.pallas_call(functools.partial(output_kernel, n), out_shape=jax.ShapeDt...  43.9 us
    unnamed x2, local copies, waits for them, and re-layouts  3.14 us

profile of v3, /device:TPU:0, one launch (start us, length us, event | category | flops | bytes accessed | tf_op | source)
XLA Modules:
  0.0 116.4 jit_solution(12235983103536937400)
XLA Ops:
  0.0 0.7 convert_element_type.10
  0.7 1.3 %reshape.41.gain = bf16[1,8192]{1,0:T(2,128)(2,1)} reshape(bf16[8192]{0:T(1024)(128)(2,1)} %param.15) | data formatting | bytes 32768 | tf_op jit(solution)/shard_map/reshape | solution.py:700
  2.0 1.5 %copy.17.adapter = s32[256,1]{1,0:T(8,128)} copy(s32[256,1]{0,1:T(1,128)} %param.26) | data formatting | bytes 2048 | tf_op args[12]
  3.5 1.5 %copy.18.lengths = s32[256,1,1]{2,1,0:T(1,128)} copy(s32[256,1,1]{0,2,1:T(1,128)} %bitcast.15) | data formatting | bytes 2048 | tf_op jit(solution)/shard_map/reshape | solution.py:704
  5.0 1.2 %fusion = (f32[256,128]{1,0:T(8,128)}, f32[256,128]{1,0:T(8,128)}) fusion(f32[128]{0:T(128)S(1)} %get-tuple-element.7, f32[128]{0:T(128)S(1)} %get-tuple-element.8, f32[256]{0:T(256)S(1)} %convert_element_type.10), kind=kLoop, calls=%fused_computation.2 | loop fusion | flops 65536 | bytes 264192 | tf_op jit(solution)/shard_map/mul | solution.py:608
  6.2 64.6 %shard_map.136.attended = bf16[128,1024]{1,0:T(8,128)(2,1)} custom-call(bf16[256,512]{1,0:T(8,128)(2,1)} %hidden.3, bf16[1,8192]{1,0:T(2,128)(2,1)} %reshape.41.gain, s32[256,1]{1,0:T(8,128)} %copy.17.adapter, f32[256,128]{1,0:T(8,128)} %get-tuple-element.6.cosine, f32[256,128]{1,0:T(8,128)} %get-tuple-element.5.sine, s32[256,1,1]{2,1,0:T(1,128)} %copy.18.lengths, ...), custom_call_target="tpu_custom_call" | custom-call | flops 2684354560 | bytes 25165824 | tf_op jit(solution)/shard_map/pallas_call | solution.py:657
  70.8 43.9 %shard_map.137 = bf16[256,512]{1,0:T(8,128)(2,1)} custom-call(bf16[256,512]{1,0:T(8,128)(2,1)} %hidden.3, bf16[128,1024]{1,0:T(8,128)(2,1)} %shard_map.136.attended, s32[256,1]{1,0:T(8,128)} %copy.17.adapter, bf16[8192,512]{1,0:T(8,128)(2,1)} %wo_hbm.1, bf16[4096,512]{1,0:T(8,128)(2,1)} %bitcast.12, bf16[4096,512]{1,0:T(8,128)(2,1)} %bitcast.13), custom_call_target="tpu_custom_call" | custom-call | flops 2147483648 | bytes 20971520 | tf_op jit(solution)/shard_map/pallas_call | solution.py:716
  114.8 1.7 %copy.21 = bf16[256,512]{1,0:T(8,128)(2,1)} copy(bf16[256,512]{1,0:T(8,128)(2,1)} %shard_map.137) | data formatting | bytes 524288
  (1 shorter events, 0.0 us)

commit v4 on v3

--- a/solution.py
+++ b/solution.py
@@ -278,7 +278,7 @@
 
 def project_kernel(
     n,
-    hidden, gain, adapter, cosine, sine, lengths,
+    hidden, gain, facts, cosine, sine,
     wq_hbm, wkv_hbm, down_hbm, upq_hbm, upkv_hbm, keys_hbm, values_hbm,
     block_out,
     q_out, kv_out, keys, values_ref, q_rows, new_keys, new_values, heads_out, buf, wq, wkv, down, upq, upkv, acc_q, acc_kv, stat, inv, own, low, pieces, low_all, q_cut, kv_cut,
@@ -321,7 +321,7 @@
             buf[block].astype(F32) * inv[:, 0:1] * gain[:, pl.ds(pl.multiple_of(block * span, span), span)].astype(F32)
         ).astype(BF16)
 
-    who = adapter[...]
+    who = facts[:, 0:1]
     own[...] = normed(me)
     loads[0].wait()
     low_partial(own[...], down, who, low)
@@ -474,11 +474,13 @@
     def some_rows(i, carry):
         at = pl.ds(pl.multiple_of(i * group, group), group)
         queries = q_rows[at]
+        ends = facts[pl.ds(pl.multiple_of(first_row + i * group, group), group), :]
+        ends = ends[:, None, :][:, :, HEAD_SIZE // 2 : HEAD_SIZE // 2 + 1]
         scores = factor * lax.dot_general(
             queries.astype(BF16), keys[at], (((2,), (2,)), ((0,), (0,))),
             preferred_element_type=F32,
         )
-        scores = jnp.where(place < lengths[pl.ds(first_row + i * group, group)], scores, -jnp.inf)
+        scores = jnp.where(place < ends, scores, -jnp.inf)
         own_score = factor * jnp.sum(queries * new_keys[at][:, None, :], axis=2, keepdims=True)
         highest = jnp.maximum(jnp.max(scores, axis=2, keepdims=True), own_score)
         weights = jnp.exp(scores - highest)
@@ -499,7 +501,7 @@
 
 def output_kernel(
     n,
-    hidden, attended, adapter, wo_hbm, down_hbm, up_hbm,
+    hidden, attended, facts, wo_hbm, down_hbm, up_hbm,
     result,
     buf, wo, down, up, acc, low, pieces, low_all,
     load_sem, zsend, ysend, csend, grecv, rs_send, rs_recv, lo_send, lo_recv,
@@ -532,7 +534,7 @@
 
     gather = Gather(n, me, view, zsend, ysend, csend, grecv)
     gather.line(0)
-    who = adapter[...]
+    who = facts[:, 0:1]
     piece = rows // n
     reduce = Exchange(
         n, me, pieces, rs_send, rs_recv,
@@ -593,7 +595,7 @@
         first_low()
         second_low()
         third_low()
-    result[...] = acc[...].astype(BF16)
+    result[...] = acc[...]
     reduce.wait_sent()
     spread.wait_sent()
     gather.wait_sent()
@@ -640,6 +642,8 @@
     slots = span // HEAD_SIZE
     dma = pltpu.SemaphoreType.DMA
     cosine, sine = rotate_tables(lengths)
+    first_half = jnp.arange(HEAD_SIZE, dtype=jnp.int32)[None, :] < HEAD_SIZE // 2
+    facts = jnp.where(first_half, adapter, lengths[:, None])
 
     def low_table(table):
         return jnp.swapaxes(table, 1, 2).reshape(-1, table.shape[1])
@@ -657,7 +661,7 @@
     block_out = pl.pallas_call(
         functools.partial(project_kernel, n),
         out_shape=jax.ShapeDtypeStruct((block_rows, GROUP_HEADS * HEAD_SIZE), BF16),
-        in_specs=[in_vmem()] * 6 + [anywhere()] * 7,
+        in_specs=[in_vmem()] * 5 + [anywhere()] * 7,
         out_specs=in_vmem(),
         scratch_shapes=[
             pltpu.VMEM((GROUP_HEADS, block_rows, HEAD_SIZE), BF16),
@@ -698,10 +702,9 @@
     )(
         hidden,
         attention_norm_gain.reshape(1, n * span),
-        adapter,
+        facts,
         cosine,
         sine,
-        lengths.reshape(rows, 1, 1),
         query_weight,
         key_value_weight,
         low_table(adapter_down_factors),
@@ -715,7 +718,7 @@
     out_low_rows = output_adapter_down.shape[0] * output_adapter_down.shape[2]
     return pl.pallas_call(
         functools.partial(output_kernel, n),
-        out_shape=jax.ShapeDtypeStruct((rows, span), BF16),
+        out_shape=jax.ShapeDtypeStruct((rows, span), F32),
         in_specs=[in_vmem()] * 3 + [anywhere()] * 3,
         out_specs=in_vmem(),
         scratch_shapes=[
@@ -738,11 +741,11 @@
     )(
         hidden,
         block_out,
-        adapter,
+        facts,
         output_weight,
         low_table(output_adapter_down),
         up_table(output_adapter_up),
-    )
+    ).astype(BF16)
 
 
 def solution(mesh):

time: 117 us -> 115 us (0.983)
  local copies, waits for them, and re-layouts: 5.96 us -> 1.34 us
  other arithmetic: 1.92 us -> 5.19 us
    unnamed x2 -> x0, local copies, waits for them, and re-layouts: 3.14 us -> none
    convert_element_type x0 -> x1, other arithmetic: none -> 1.78 us  [body(): return pl.pallas_call(functools.partial(output_kernel, n), out_shape=jax....]
    select_n x1, other arithmetic: 0.01 us -> 1.48 us  [body(): facts = jnp.where(first_half, adapter, lengths[:, None])]
    reshape x1 -> x0, local copies, waits for them, and re-layouts: 1.47 us -> none  [body(): lengths.reshape(rows, 1, 1)]
where the time goes in v4:
time: 115 us
  Pallas kernels  109 us (95%)
  other arithmetic  5.19 us (5%)
  local copies, waits for them, and re-layouts  1.34 us (1%)
    pallas_call x1, Pallas kernels, body(): pl.pallas_call(functools.partial(project_kernel, n), out_shape=jax.ShapeD...  64.6 us
    pallas_call x1, Pallas kernels, body(): pl.pallas_call(functools.partial(output_kernel, n), out_shape=jax.ShapeDt...  44 us

profile of v4, /device:TPU:0, one launch (start us, length us, event | category | flops | bytes accessed | tf_op | source)
XLA Modules:
  0.0 115.2 jit_solution(17240542540630916392)
XLA Ops:
  0.0 0.7 convert_element_type.13
  0.7 1.3 %reshape.42.gain = bf16[1,8192]{1,0:T(2,128)(2,1)} reshape(bf16[8192]{0:T(1024)(128)(2,1)} %param.15) | data formatting | bytes 32768 | tf_op jit(solution)/shard_map/reshape | solution.py:704
  2.0 1.5 %broadcast_select_fusion.facts = s32[256,128]{1,0:T(8,128)} fusion(s32[256]{0:T(256)} %param.27, s32[256]{0:T(256)} %bitcast.15, pred[128]{0:T(512)(128)(4,1)S(1)} %iota_compare_fusion), kind=kLoop, calls=%fused_computation.3 | loop fusion | flops 32768 | bytes 133248 | tf_op jit(solution)/shard_map/jit(_where)/select_n | solution.py:646
  3.5 1.2 %fusion = (f32[256,128]{1,0:T(8,128)}, f32[256,128]{1,0:T(8,128)}) fusion(f32[128]{0:T(128)S(1)} %get-tuple-element.8, f32[128]{0:T(128)S(1)} %get-tuple-element.7, f32[256]{0:T(256)S(1)} %convert_element_type.13), kind=kLoop, calls=%fused_computation.2 | loop fusion | flops 65536 | bytes 264192 | tf_op jit(solution)/shard_map/mul | solution.py:610
  4.8 64.6 %shard_map.136.attended = bf16[128,1024]{1,0:T(8,128)(2,1)} custom-call(bf16[256,512]{1,0:T(8,128)(2,1)} %hidden.3, bf16[1,8192]{1,0:T(2,128)(2,1)} %reshape.42.gain, s32[256,128]{1,0:T(8,128)} %broadcast_select_fusion.facts, f32[256,128]{1,0:T(8,128)} %get-tuple-element.6.cosine, f32[256,128]{1,0:T(8,128)} %get-tuple-element.5.sine, ...), custom_call_target="tpu_custom_call" | custom-call | flops 2684354560 | bytes 25165824 | tf_op jit(solution)/shard_map/pallas_call | solution.py:661
  69.4 44.0 %shard_map.137 = f32[256,512]{1,0:T(8,128)} custom-call(bf16[256,512]{1,0:T(8,128)(2,1)} %hidden.3, bf16[128,1024]{1,0:T(8,128)(2,1)} %shard_map.136.attended, s32[256,128]{1,0:T(8,128)} %broadcast_select_fusion.facts, bf16[8192,512]{1,0:T(8,128)(2,1)} %wo_hbm.1, bf16[4096,512]{1,0:T(8,128)(2,1)} %bitcast.12, bf16[4096,512]{1,0:T(8,128)(2,1)} %bitcast.13), custom_call_target="tpu_custom_call" | custom-call | flops 2147483648 | bytes 20971520 | tf_op jit(solution)/shard_map/pallas_call | solution.py:719
  113.4 1.8 %convert_element_type.15 = bf16[256,512]{1,0:T(8,128)(2,1)} convert(f32[256,512]{1,0:T(8,128)} %shard_map.137) | non-fusion elementwise | flops 131072 | bytes 786432 | tf_op jit(solution)/shard_map/convert_element_type | solution.py:748
  (2 shorter events, 0.0 us)
